TPU v7x, 128 devices: a whole 4x4x4 slice. The times are simulated.
128 devices in a mesh: ctx: 32 (over z, y_hi, x), wa: 4 (over y_lo, core).
Axes of the slice: x: 4, y: 4 (y_hi: 2, y_lo: 2; y = y_hi * 2 + y_lo), z: 4, core: 2. Of those that a mesh axis runs over, the one named last changes fastest.
Arguments:
- tokens: bfloat16 [4096, 8192], P('ctx', 'wa')
- norm_gain: bfloat16 [8192], P('wa'), may hold values from 0.5 to 1.5
- w_query: bfloat16 [8192, 4096], P('wa'), may hold values from -0.0625 to 0.0625
- keyvalue_weight: bfloat16 [8192, 1024], P('wa'), may hold values from -0.0625 to 0.0625
- cache_keyval: bfloat16 [65536, 1024], P('ctx', 'wa')
- kept_blocks: int32 [32, 3], P('ctx'), may hold values from 0 to 15, as said below
- kept_counts: int32 [32], P('ctx'), may hold values from 1 to 3, as said below
Outputs:
- attended: bfloat16 [4096, 4096], P('ctx', 'wa')
Inputs may be any that keep to these rules, and one draw needn't show every extreme that they name: `kept_blocks`: within one row the indices are distinct. `kept_counts`: some shard uses exactly 3 slots.
All inputs are finite; a program needn't handle non-finite values.
Results may differ from a plain program's by a relative error of at most 0.0095.
The roundings to bfloat16 on the way count: a program that leaves them out, or rounds other values in their place, can miss the bound.
Values may be sent and summed in bfloat16 or wider, within the bound.
No kernel may reach another device: no remote copies, remote signals or barrier semaphores. Data moves between devices by JAX's collectives and lax.ppermute only.
A program may use at most 192 MiB of HBM per device.

v0:
```python
import math

import jax
import jax.numpy as jnp
from jax import lax
from jax.sharding import PartitionSpec as P

HEAD_WIDTH = 128
BLOCK = 128
MAXB = 3


def attend(carry, kv_rows, visible, queries_four):
    top, total, summed = carry
    heads_local = queries_four.shape[1]
    rows_block = kv_rows.reshape(kv_rows.shape[0], heads_local, 2, HEAD_WIDTH)
    keys_part = rows_block[:, :, 0, :]
    values_part = rows_block[:, :, 1, :]
    scores = jnp.einsum(
        "thgd,khd->htgk", queries_four, keys_part, preferred_element_type=jnp.float32
    )
    mask_full = visible[None, :, None, :]
    masked = jnp.where(mask_full, scores, -1e30)
    new_top = jnp.maximum(top, jnp.max(masked, axis=-1))
    weights = jnp.where(mask_full, jnp.exp(masked - new_top[..., None]), 0.0)
    factor = jnp.exp(top - new_top)
    total = total * factor + jnp.sum(weights, axis=-1)
    mixed = jnp.einsum(
        "htgk,khd->htgd",
        weights.astype(jnp.bfloat16),
        values_part,
        preferred_element_type=jnp.float32,
    )
    summed = summed * factor[..., None] + mixed
    return (new_top, total, summed)


def fold_rows(carry, kv_rows, mask_maker, queries_four):
    count_rows = kv_rows.shape[0]
    width_block = math.gcd(count_rows, 512)

    def advance(position, state):
        offset = position * width_block
        rows_now = lax.dynamic_slice_in_dim(kv_rows, offset, width_block, 0)
        visible = mask_maker(offset, offset, width_block)
        return attend(state, rows_now, visible, queries_four)

    return lax.fori_loop(0, count_rows // width_block, advance, carry)


def on_device(tokens, norm_gain, w_query, keyvalue_weight, cache_keyval, kept_blocks, kept_counts):
    tok_rows = tokens.shape[0]
    whole, gain_whole = (
        lax.all_gather(tokens, "wa", axis=1, tiled=True),
        lax.all_gather(norm_gain, "wa", axis=0, tiled=True),
    )
    values = whole.astype(jnp.float32)
    meansq = jnp.mean(values * values, axis=1, keepdims=True)
    normed = (values * lax.rsqrt(meansq + 1e-05) * gain_whole.astype(jnp.float32)[None, :]).astype(
        jnp.bfloat16
    )
    query_cols, keyval_cols = (
        lax.all_to_all(w_query, "wa", split_axis=1, concat_axis=0, tiled=True),
        lax.all_to_all(keyvalue_weight, "wa", split_axis=1, concat_axis=0, tiled=True),
    )
    query_sum = jnp.dot(normed, query_cols, preferred_element_type=jnp.float32)
    keyval_sum = jnp.dot(normed, keyval_cols, preferred_element_type=jnp.float32)
    queries = (query_sum * HEAD_WIDTH ** (-0.5)).astype(jnp.bfloat16)
    new_keyval = keyval_sum.astype(jnp.bfloat16)
    heads_local = new_keyval.shape[1] // (2 * HEAD_WIDTH)
    head_group = queries.shape[1] // (heads_local * HEAD_WIDTH)
    queries_four = queries.reshape(tok_rows, heads_local, head_group, HEAD_WIDTH)
    width_local = cache_keyval.shape[1]
    block_count = cache_keyval.shape[0] // BLOCK
    picked = cache_keyval.reshape(block_count, BLOCK, width_local)[kept_blocks[0]]
    kept_rows = picked.reshape(MAXB * BLOCK, width_local)
    slot_ids = jnp.arange(MAXB * BLOCK) // BLOCK
    live_flags = (slot_ids < kept_counts[0]).astype(jnp.bfloat16)
    my_shard = lax.axis_index("ctx")
    query_index = my_shard * tok_rows + jnp.arange(tok_rows)
    init = (
        jnp.full((heads_local, tok_rows, head_group), -1e30, jnp.float32),
        jnp.zeros((heads_local, tok_rows, head_group), jnp.float32),
        jnp.zeros((heads_local, tok_rows, head_group, HEAD_WIDTH), jnp.float32),
    )
    rows_piece = lax.all_gather(kept_rows, "ctx", axis=0, tiled=True)
    live_piece = lax.all_gather(live_flags, "ctx", axis=0, tiled=True)

    def cache_mask(global_start, offset, width_block):
        live_now = lax.dynamic_slice_in_dim(live_piece, offset, width_block, 0) > 0
        return jnp.broadcast_to(live_now[None, :], (tok_rows, width_block))

    carried = fold_rows(init, rows_piece, cache_mask, queries_four)

    def span_mask(global_start, offset, width_block):
        key_index = global_start + jnp.arange(width_block)
        return key_index[None, :] <= query_index[:, None]

    carried = fold_rows(
        carried, lax.all_gather(new_keyval, "ctx", axis=0, tiled=True), span_mask, queries_four
    )
    final_top, final_total, final_sum = carried
    result = final_sum / final_total[..., None]
    result = jnp.transpose(result, (1, 0, 2, 3)).reshape(
        tok_rows, heads_local * head_group * HEAD_WIDTH
    )
    return result.astype(jnp.bfloat16)


def solution(mesh):
    return jax.shard_map(
        on_device,
        mesh=mesh,
        in_specs=(
            P("ctx", "wa"),
            P("wa"),
            P("wa", None),
            P("wa", None),
            P("ctx", "wa"),
            P("ctx", None),
            P("ctx"),
        ),
        out_specs=P("ctx", "wa"),
        check_vma=False,
    )
```

profile of v0, /device:TPU:0, one launch (start us, length us, event | category | flops | bytes accessed | tf_op | source)
XLA Modules:
  0.0 598.3 jit_solution(6876186711223215149)
XLA Ops:
  6.5 6.6 %copy.48 = bf16[2048,1024]{0,1:T(8,128)(2,1)} copy(bf16[2048,1024]{1,0:T(8,128)(2,1)} %param.14) | data formatting | bytes 8388608 | tf_op args[3]
  13.1 4.9 all-to-all-start.1
  18.7 22.6 %copy.44 = bf16[2048,4096]{0,1:T(8,128)(2,1)} copy(bf16[2048,4096]{1,0:T(8,128)(2,1)} %param.13) | data formatting | bytes 33554432 | tf_op args[2]
  41.3 41.8 %all-to-all-done.1 = bf16[2048,4,256]{0,2,1:T(8,128)(2,1)} async-done(((bf16[2048,4,256]{0,2,1:T(8,128)(2,1)}), bf16[2048,4,256]{0,2,1:T(8,128)(2,1)}, u32[]{:S(2)}, u32[]{:S(2)}) %all-to-all-start.1) | async-done | bytes 4194336 | tf_op jit(solution)/shard_map/all_to_all | solution.py:64
  83.1 7.1 %all-to-all-start = ((bf16[2048,4,1024]{0,2,1:T(8,128)(2,1)}), bf16[2048,4,1024]{0,2,1:T(8,128)(2,1)}, u32[]{:S(2)}, u32[]{:S(2)}) async-start(bf16[2048,4,1024]{0,2,1:T(8,128)(2,1)} %bitcast.159), calls=%async_computation | async-start | bytes 33554432 | tf_op jit(solution)/shard_map/all_to_all | solution.py:63
  90.3 1.2 gather_fusion
  91.6 212.0 %all_gather.18 = bf16[8192]{0:T(1024)(128)(2,1)S(1)} all-gather(bf16[2048]{0:T(1024)(128)(2,1)S(1)} %copy-done.5), channel_id=1, replica_groups=mesh['ctx'=32,'wa'=4] {'wa'}, dimensions={0}, use_global_device_ids=true | all-gather | bytes 20480 | tf_op jit(solution)/shard_map/all_gather | solution.py:55
  304.3 96.4 %all-gather = bf16[32,1,384]{2,1,0:T(2,128)(2,1)S(1)} all-gather(bf16[1,1,384]{2,1,0:T(2,128)(2,1)S(1)} %reshape.207), channel_id=1, replica_groups=mesh['ctx'=32,'wa'=4] {'ctx'}, dimensions={0}, use_global_device_ids=true | all-gather | bytes 25344 | tf_op jit(solution)/shard_map/all_gather | solution.py:87
  400.9 6.2 %copy.49 = bf16[4,2048,256]{2,1,0:T(8,128)(2,1)} copy(bf16[4,2048,256]{1,2,0:T(8,128)(2,1)} %bitcast.9) | data formatting | bytes 8388608 | tf_op jit(solution)/shard_map/all_to_all | solution.py:64
  407.2 2.2 fusion.32
  409.4 3.6 convolution_convert_fusion
  413.0 22.6 %copy.45 = bf16[4,2048,1024]{2,1,0:T(8,128)(2,1)} copy(bf16[4,2048,1024]{1,2,0:T(8,128)(2,1)} %bitcast.6) | data formatting | bytes 33554432 | tf_op jit(solution)/shard_map/all_to_all | solution.py:63
  435.6 8.2 %fusion.36 = bf16[16,8,8,128]{3,1,2,0:T(8,128)(2,1)S(1)} fusion(bf16[8192,1024]{1,0:T(8,128)(2,1)} %bitcast.160, bf16[128,8192]{1,0:T(8,128)(2,1)S(1)} %copy-done.2, f32[8192]{0:T(1024)S(1)} %convert_element_type.42, f32[128]{0:T(128)S(1)} %add_rsqrt_fusion), kind=kOutput, calls=%fused_computation.61 | convolution fusion | flops 2151940096 | bytes 19169792 | tf_op jit(solution)/shard_map/dot_general | solution.py:66
  444.0 117.9 %while.37 = (s32[]{:T(128)}, f32[1,128,8]{1,2,0:T(8,128)S(1)}, f32[1,128,8]{1,2,0:T(8,128)S(1)}, f32[1,128,8,128]{3,1,2,0:T(8,128)}, bf16[12288]{0:T(1024)(128)(...) while((s32[]{:T(128)}, f32[1,128,8]{1,2,0:T(8,128)S(1)}, ...), condition=%wide.region_4.5_spmd.clone, body=%wide.region_1.4_spmd.clone.sunk | while | flops 274079232 | bytes 8982191 | solution.py:48
  444.1 1.0 constant_dynamic-slice_fusion.5
  445.7 1.6 fusion.64
  448.0 1.0 constant_dynamic-slice_fusion.5
  449.7 2.7 fusion.64
  453.0 1.0 constant_dynamic-slice_fusion.5
  454.6 2.7 fusion.64
  457.9 1.0 constant_dynamic-slice_fusion.5
  459.6 2.7 fusion.64
  462.9 1.0 constant_dynamic-slice_fusion.5
  464.5 2.7 fusion.64
  467.9 1.0 constant_dynamic-slice_fusion.5
  469.5 2.7 fusion.64
  472.8 1.0 constant_dynamic-slice_fusion.5
  474.4 2.7 fusion.64
  477.8 1.0 constant_dynamic-slice_fusion.5
  479.4 2.7 fusion.64
  482.7 1.0 constant_dynamic-slice_fusion.5
  484.3 2.7 fusion.64
  487.7 1.0 constant_dynamic-slice_fusion.5
  489.3 2.7 fusion.64
  492.6 1.0 constant_dynamic-slice_fusion.5
  494.3 2.7 fusion.64
  497.6 1.0 constant_dynamic-slice_fusion.5
  499.2 2.7 fusion.64
  504.2 2.7 fusion.64
  509.1 2.7 fusion.64
  514.1 2.7 fusion.64
  519.0 2.7 fusion.64
  524.0 2.7 fusion.64
  527.3 1.0 constant_dynamic-slice_fusion.5
  528.9 2.7 fusion.64
  533.9 2.7 fusion.64
  537.2 1.0 constant_dynamic-slice_fusion.5
  538.9 2.7 fusion.64
  543.8 2.7 fusion.64
  547.2 1.0 constant_dynamic-slice_fusion.5
  548.8 2.7 fusion.64
  553.7 2.7 fusion.64
  557.1 1.0 constant_dynamic-slice_fusion.5
  558.7 2.7 fusion.64
  562.0 27.5 %while.36 = (s32[]{:T(128)}, f32[1,128,8]{1,2,0:T(8,128)S(1)}, f32[1,128,8]{1,2,0:T(8,128)S(1)}, f32[1,128,8,128]{3,1,2,0:T(8,128)}, bf16[4096,256]{1,0:T(8,128)...) while((s32[]{:T(128)}, f32[1,128,8]{1,2,0:T(8,128)S(1)}, ...), condition=%wide.region_8.9_spmd.clone, body=%wide.region_5.8_spmd.clone.sunk | while | flops 274009728 | bytes 13440223 | solution.py:48
  562.0 1.0 constant_dynamic-slice_fusion.4
  565.4 1.0 constant_dynamic-slice_fusion.4
  568.9 1.0 constant_dynamic-slice_fusion.4
  572.3 1.0 constant_dynamic-slice_fusion.4
  575.7 1.0 constant_dynamic-slice_fusion.4
  579.2 1.0 constant_dynamic-slice_fusion.4
  582.6 1.0 constant_dynamic-slice_fusion.4
  586.0 1.0 constant_dynamic-slice_fusion.4
  589.5 1.3 divide_convert_fusion
  (323 shorter events, 58.4 us)
Async XLA Ops:
  6.5 83.7 %copy-start = (bf16[2048,256]{1,0:T(8,128)(2,1)S(1)}, bf16[2048,256]{1,0:T(8,128)(2,1)}, u32[]{:S(2)}) copy-start(bf16[2048,256]{1,0:T(8,128)(2,1)} %param.15) | copy-start | bytes 3145732
  13.1 70.0 %all-to-all-start.1 = ((bf16[2048,4,256]{0,2,1:T(8,128)(2,1)}), bf16[2048,4,256]{0,2,1:T(8,128)(2,1)}, u32[]{:S(2)}, u32[]{:S(2)}) async-start(bf16[2048,4,256]{0,2,1:T(8,128)(2,1)} %bitcast.161), calls=%async_computation.1 | async-start | bytes 8388608 | tf_op jit(solution)/shard_map/all_to_all | solution.py:64
  18.0 389.2 %all-gather.7.cloned.1.call-start = ((), (), s32[]{:S(2)}) async-start(), calls=%async_computation.3 | async-start | bytes 2621440 | tf_op jit(solution)/shard_map/all_gather | solution.py:54
  83.1 7.2 %copy-start.6 = (s32[1,3]{1,0:T(1,128)S(1)}, s32[1,3]{1,0:T(1,128)}, u32[]{:S(2)}) copy-start(s32[1,3]{1,0:T(1,128)} %param.16) | copy-start | bytes 40
  83.1 8.6 %copy-start.5 = (bf16[2048]{0:T(1024)(128)(2,1)S(1)}, bf16[2048]{0:T(1024)(128)(2,1)}, u32[]{:S(2)}) copy-start(bf16[2048]{0:T(1024)(128)(2,1)} %param.12) | copy-start | bytes 12292
  83.1 329.9 %all-to-all-start = ((bf16[2048,4,1024]{0,2,1:T(8,128)(2,1)}), bf16[2048,4,1024]{0,2,1:T(8,128)(2,1)}, u32[]{:S(2)}, u32[]{:S(2)}) async-start(bf16[2048,4,1024]{0,2,1:T(8,128)(2,1)} %bitcast.159), calls=%async_computation | async-start | bytes 33554432 | tf_op jit(solution)/shard_map/all_to_all | solution.py:63
  90.2 353.8 %all-gather.5.cloned.1.call-start = ((), (), s32[]{:S(2)}) async-start(), calls=%async_computation.2 | async-start | bytes 6488064 | tf_op jit(solution)/shard_map/all_gather | solution.py:86
  91.5 470.4 %all-gather.9.cloned.1.call-start = ((), (), s32[]{:S(2)}) async-start(), calls=%async_computation.4 | async-start | bytes 2162688 | tf_op jit(solution)/shard_map/all_gather | solution.py:100
  407.2 2.2 copy-start.2
  562.0 1.9 copy-start.3
  564.6 0.8 copy-start.4
  565.4 1.8 copy-start.3
  568.1 0.8 copy-start.4
  568.9 1.8 copy-start.3
  571.5 0.8 copy-start.4
  572.3 1.8 copy-start.3
  574.9 0.8 copy-start.4
  575.7 1.8 copy-start.3
  578.4 0.8 copy-start.4
  579.2 1.8 copy-start.3
  581.8 0.8 copy-start.4
  582.6 1.8 copy-start.3
  585.2 0.8 copy-start.4
  586.0 1.8 copy-start.3
  588.7 0.8 copy-start.4
  589.5 2.3 copy-start.1
Sparse Core Ops, SparseCore 0:
  20.5 49.3 all-gather.6
  94.0 125.0 all-gather.4
  413.1 64.2 all-gather.8
where the time goes:
time: 602 us; the launch traced here: 598 us
  blocking collectives  308 us (51%)
  local copies, waits for them, and re-layouts  98.8 us (16%)
  matrix products  96.4 us (16%)
  waiting for transfers between devices  42.5 us (7%)
  other arithmetic  23.7 us (4%)
  between operations  14 us (2%)
  starting transfers between devices  12.1 us (2%)
    all_gather x1, blocking collectives, on_device(): lax.all_gather(norm_gain, 'wa', axis=0, tiled=True)  212 us
    all_gather x1, blocking collectives, on_device(): live_piece = lax.all_gather(live_flags, 'ctx', axis=0, tiled=True)  96.4 us
    dot_general x32, matrix products, attend(): jnp.einsum('htgk,khd->htgd', weights.astype(jnp.bfloat16), values_part, p...  69.4 us
    all_to_all x1, waiting for transfers between devices, on_device(): lax.all_to_all(keyvalue_weight, 'wa', split_axis=1, concat_axis=0, tiled=...  41.8 us
    dynamic_slice x64, local copies, waits for them, and re-layouts, advance(): rows_now = lax.dynamic_slice_in_dim(kv_rows, offset, width_block, 0)  35.9 us
    unnamed x17, local copies, waits for them, and re-layouts  30 us
    all_to_all x1, local copies, waits for them, and re-layouts, on_device(): lax.all_to_all(w_query, 'wa', split_axis=1, concat_axis=0, tiled=True)  22.6 us
    reduce_sum x32, other arithmetic, attend(): total = total * factor + jnp.sum(weights, axis=-1)  16.2 us
  transfers between devices with their start and end apart: 5, of which 1 were waited for; matrix products, arithmetic and copies ran while one was open for 31% of the time, Pallas kernels for 0%

commit v1 on v0

v1 whole, which is shorter than its diff:
```python
import functools

import jax
import jax.numpy as jnp
from jax import lax
from jax.experimental import pallas as pl
from jax.experimental.pallas import tpu as pltpu
from jax.sharding import PartitionSpec as P

HEAD = 128
BLOCK = 128
MAXB = 3
GROUP = 8
TOK = 128
WIDTH = 8192
PEERS = 16
ROWS_SENT = MAXB * BLOCK + 16
KC = 512
RC = 256
NEG = -1e30

NT = (((1,), (1,)), ((), ()))
NN = (((1,), (0,)), ((), ()))


def plane_groups():
    return [[z * 8 + y * 4 + x for z in range(4) for x in range(4)] for y in range(2)]


def gather_plane(rows):
    copies = jnp.broadcast_to(rows[None], (PEERS,) + rows.shape)
    return lax.all_to_all(
        copies, "ctx", split_axis=0, concat_axis=0, axis_index_groups=plane_groups()
    )


def project_kernel(me_ref, tok_ref, gain_ref, ss_ref, wq_ref, wkv_ref, send_ref, keep_ref, normed):
    i, j = pl.program_id(0), pl.program_id(1)

    @pl.when((i == 0) & (j == 0))
    def _():
        scale = lax.rsqrt(ss_ref[...] * (1.0 / WIDTH) + 1e-05)
        values = tok_ref[...].astype(jnp.float32) * scale
        normed[...] = (values * gain_ref[...].astype(jnp.float32)).astype(jnp.bfloat16)

    q_part = jnp.dot(normed[...], wq_ref[...], preferred_element_type=jnp.float32)
    kv_part = jnp.dot(normed[...], wkv_ref[...], preferred_element_type=jnp.float32)
    for jj in range(2):

        @pl.when((i < 2) & (j == jj))
        def _():
            send_ref[0, :, jj * 512 : (jj + 1) * 512] = q_part
            send_ref[0, :, 1024 + jj * 128 : 1024 + (jj + 1) * 128] = kv_part

        @pl.when((i >= 2) & (j == jj))
        def _():
            keep_ref[0, :, jj * 512 : (jj + 1) * 512] = q_part
            keep_ref[0, :, 1024 + jj * 128 : 1024 + (jj + 1) * 128] = kv_part


def project(me, tokens, gain, sumsq, w_query, keyvalue_weight):
    def column(i, me_ref):
        rel = jnp.where(i == 0, 3, jnp.where(i == 1, 1, jnp.where(i == 2, 2, 0)))
        return me_ref[0] ^ rel

    shape = jax.ShapeDtypeStruct((2, TOK, 1280), jnp.float32)
    return pl.pallas_call(
        project_kernel,
        out_shape=(shape, shape),
        grid_spec=pltpu.PrefetchScalarGridSpec(
            num_scalar_prefetch=1,
            grid=(4, 2),
            in_specs=[
                pl.BlockSpec((TOK, 2048), lambda i, j, m: (0, 0)),
                pl.BlockSpec((1, 2048), lambda i, j, m: (0, 0)),
                pl.BlockSpec((TOK, 1), lambda i, j, m: (0, 0)),
                pl.BlockSpec((2048, 512), lambda i, j, m: (0, column(i, m) * 2 + j)),
                pl.BlockSpec((2048, 128), lambda i, j, m: (0, column(i, m) * 2 + j)),
            ],
            out_specs=[
                pl.BlockSpec((1, TOK, 1280), lambda i, j, m: (jnp.minimum(i, 1), 0, 0)),
                pl.BlockSpec((1, TOK, 1280), lambda i, j, m: (jnp.maximum(i - 2, 0), 0, 0)),
            ],
            scratch_shapes=[pltpu.VMEM((TOK, 2048), jnp.bfloat16)],
        ),
        compiler_params=pltpu.CompilerParams(vmem_limit_bytes=24 * 2**20),
        cost_estimate=pl.CostEstimate(
            flops=2 * TOK * 2048 * 5120, transcendentals=0, bytes_accessed=24 * 2**20
        ),
    )(me, tokens, gain.reshape(1, 2048), sumsq, w_query, keyvalue_weight)


def fold(q_ref, rows, first, kv, offset, top_ref, acc_ref, visible=None):
    keys = kv[pl.ds(offset, KC), 0:HEAD]
    values = kv[pl.ds(offset, KC), HEAD : 3 * HEAD]
    steps = rows // RC

    def score(r):
        s = lax.dot_general(
            q_ref[first + r * RC : first + (r + 1) * RC, :],
            keys,
            NT,
            preferred_element_type=jnp.float32,
        )
        return s if visible is None else jnp.where(visible, s, NEG)

    following = score(0)
    for r in range(steps):
        s = following
        if r + 1 < steps:
            following = score(r + 1)
        where = slice(first + r * RC, first + (r + 1) * RC)
        before = top_ref[where, :]
        top = jnp.maximum(before, jnp.max(s, axis=1, keepdims=True))
        weights = jnp.exp(s - top[:, 0:1])
        factor = jnp.exp(before - top)
        mixed = lax.dot_general(
            weights.astype(jnp.bfloat16), values, NN, preferred_element_type=jnp.float32
        )
        top_ref[where, :] = top
        acc_ref[where, 0:HEAD] = acc_ref[where, 0:HEAD] * factor + mixed[:, 0:HEAD]
        acc_ref[where, HEAD:] = acc_ref[where, HEAD:] * factor + mixed[:, HEAD:]


def stack_heads(q_ref, dst, first):
    for g in range(GROUP):
        dst[first + g * TOK : first + (g + 1) * TOK, :] = q_ref[:, g * HEAD : (g + 1) * HEAD]


def cached_kernel(counts_ref, qo_ref, qp_ref, kv_ref, acc_ref, top_ref, q_all, kv, sems):
    def copies(act):
        position = jnp.int32(0)
        for shard in range(PEERS):
            count = counts_ref[shard]
            for slot in range(MAXB):

                @pl.when(slot < count)
                def _():
                    act(
                        pltpu.make_async_copy(
                            kv_ref.at[shard, pl.ds(slot * BLOCK, BLOCK), :],
                            kv.at[pl.ds(pl.multiple_of((position + slot) * BLOCK, BLOCK), BLOCK), 0 : 2 * HEAD],
                            sems.at[shard * MAXB + slot],
                        )
                    )

            position = position + count
        return position

    live = copies(lambda c: c.start())
    for b in range(KC // BLOCK - 1):
        kv[pl.ds(pl.multiple_of((live + b) * BLOCK, BLOCK), BLOCK), 0 : 2 * HEAD] = jnp.zeros(
            (BLOCK, 2 * HEAD), jnp.bfloat16
        )
    kv[:, 2 * HEAD :] = jnp.ones((kv.shape[0], HEAD), jnp.bfloat16)
    stack_heads(qo_ref, q_all, 0)
    stack_heads(qp_ref, q_all, GROUP * TOK)
    top_ref[...] = jnp.full_like(top_ref, NEG)
    acc_ref[...] = jnp.zeros_like(acc_ref)
    copies(lambda c: c.wait())

    rows = 2 * GROUP * TOK
    chunks = (live * BLOCK + KC - 1) // KC

    def step(c, _):
        fold(q_all, rows, 0, kv, pl.multiple_of(c * KC, KC), top_ref, acc_ref)
        return 0

    lax.fori_loop(0, chunks - 1, step, 0)
    last = (chunks - 1) * KC
    column = lax.broadcasted_iota(jnp.int32, (RC, KC), 1)
    fold(q_all, rows, 0, kv, pl.multiple_of(last, KC), top_ref, acc_ref, column < live * BLOCK - last)


def attend_cached(counts, q_own, q_other, kv):
    rows = 2 * GROUP * TOK
    vmem = pl.BlockSpec(memory_space=pltpu.VMEM)
    return pl.pallas_call(
        cached_kernel,
        out_shape=(
            jax.ShapeDtypeStruct((rows, 2 * HEAD), jnp.float32),
            jax.ShapeDtypeStruct((rows, HEAD), jnp.float32),
        ),
        in_specs=[pl.BlockSpec(memory_space=pltpu.SMEM), vmem, vmem, pl.BlockSpec(memory_space=pl.ANY)],
        out_specs=(vmem, vmem),
        scratch_shapes=[
            pltpu.VMEM((rows, HEAD), jnp.bfloat16),
            pltpu.VMEM((PEERS * MAXB * BLOCK + KC, 3 * HEAD), jnp.bfloat16),
            pltpu.SemaphoreType.DMA((PEERS * MAXB,)),
        ],
        compiler_params=pltpu.CompilerParams(vmem_limit_bytes=40 * 2**20),
        cost_estimate=pl.CostEstimate(
            flops=4 * rows * 4096 * 256, transcendentals=rows * 4096, bytes_accessed=8 * 2**20
        ),
    )(counts, q_own, q_other, kv)


def span_kernel(own, info_ref, q_ref, kv_ref, acc_in, top_in, out_ref, log_ref, q_all, kv, acc, top, sems):
    chunks = info_ref[0]

    def copy(c):
        return pltpu.make_async_copy(
            kv_ref.at[pl.ds(c * KC, KC), :], kv.at[pl.ds(c * KC, KC), 0 : 2 * HEAD], sems.at[c]
        )

    last = chunks if own else chunks - 1
    for c in range(4):

        @pl.when(c <= last)
        def _():
            copy(c).start()

    kv[:, 2 * HEAD :] = jnp.ones((kv.shape[0], HEAD), jnp.bfloat16)
    stack_heads(q_ref, q_all, 0)
    acc[...] = acc_in[...]
    top[...] = top_in[...]
    for c in range(4):

        @pl.when(c <= last)
        def _():
            copy(c).wait()

    rows = GROUP * TOK

    def step(c, _):
        fold(q_all, rows, 0, kv, pl.multiple_of(c * KC, KC), top, acc)
        return 0

    lax.fori_loop(0, chunks, step, 0)
    if own:
        column = lax.broadcasted_iota(jnp.int32, (RC, KC), 1)
        token = lax.broadcasted_iota(jnp.int32, (RC, KC), 0) % TOK
        visible = column <= token + info_ref[1] * TOK
        fold(q_all, rows, 0, kv, pl.multiple_of(chunks * KC, KC), top, acc, visible)

    lane = lax.broadcasted_iota(jnp.int32, (TOK, HEAD), 1)
    logs = jnp.zeros((TOK, HEAD), jnp.float32)
    for g in range(GROUP):
        where = slice(g * TOK, (g + 1) * TOK)
        total = acc[where, HEAD:]
        out = acc[where, 0:HEAD] / total
        out_ref[:, g * HEAD : (g + 1) * HEAD] = out.astype(out_ref.dtype)
        log = top[where, :] + jnp.log(total)
        if own:
            logs = jnp.where(lane == g, log, logs)
        else:
            high = log.astype(jnp.bfloat16).astype(jnp.float32)
            middle = (log - high).astype(jnp.bfloat16).astype(jnp.float32)
            low = log - high - middle
            logs = jnp.where(lane == g, high, logs)
            logs = jnp.where(lane == GROUP + g, middle, logs)
            logs = jnp.where(lane == 2 * GROUP + g, low, logs)
    if own:
        log_ref[...] = logs
    else:
        out_ref[:, GROUP * HEAD :] = logs.astype(jnp.bfloat16)


def attend_span(own, info, q, kv, acc, top):
    rows = GROUP * TOK
    half = 0 if own else 1
    vmem = pl.BlockSpec(memory_space=pltpu.VMEM)
    if own:
        outs = (
            jax.ShapeDtypeStruct((TOK, GROUP * HEAD), jnp.float32),
            jax.ShapeDtypeStruct((TOK, HEAD), jnp.float32),
        )
        kernel = functools.partial(span_kernel, True)
    else:
        outs = (jax.ShapeDtypeStruct((TOK, (GROUP + 1) * HEAD), jnp.bfloat16),)

        def kernel(info_ref, q_ref, kv_ref, acc_in, top_in, out_ref, *scratch):
            span_kernel(False, info_ref, q_ref, kv_ref, acc_in, top_in, out_ref, None, *scratch)

    return pl.pallas_call(
        kernel,
        out_shape=outs,
        grid=(1,),
        in_specs=[
            pl.BlockSpec(memory_space=pltpu.SMEM),
            pl.BlockSpec((TOK, GROUP * HEAD), lambda i: (0, 0)),
            pl.BlockSpec(memory_space=pl.ANY),
            pl.BlockSpec((rows, 2 * HEAD), lambda i: (half, 0)),
            pl.BlockSpec((rows, HEAD), lambda i: (half, 0)),
        ],
        out_specs=tuple(pl.BlockSpec(o.shape, lambda i: (0, 0)) for o in outs),
        scratch_shapes=[
            pltpu.VMEM((rows, HEAD), jnp.bfloat16),
            pltpu.VMEM((4 * KC, 3 * HEAD), jnp.bfloat16),
            pltpu.VMEM((rows, 2 * HEAD), jnp.float32),
            pltpu.VMEM((rows, HEAD), jnp.float32),
            pltpu.SemaphoreType.DMA((4,)),
        ],
        compiler_params=pltpu.CompilerParams(vmem_limit_bytes=32 * 2**20),
        cost_estimate=pl.CostEstimate(
            flops=4 * rows * 2048 * 256, transcendentals=rows * 2048, bytes_accessed=4 * 2**20
        ),
    )(info, q, kv, acc, top)


def join_kernel(own_ref, log_ref, other_ref, out_ref):
    for g in range(GROUP):
        where = slice(g * HEAD, (g + 1) * HEAD)
        mine = log_ref[:, g : g + 1]
        base = GROUP * HEAD
        theirs = other_ref[:, base + g : base + g + 1].astype(jnp.float32)
        for part in (1, 2):
            at = base + part * GROUP + g
            theirs = theirs + other_ref[:, at : at + 1].astype(jnp.float32)
        share = 1.0 / (1.0 + jnp.exp(theirs - mine))
        rest = 1.0 / (1.0 + jnp.exp(mine - theirs))
        out = own_ref[:, where] * share + other_ref[:, where].astype(jnp.float32) * rest
        out_ref[:, where] = out.astype(jnp.bfloat16)


def join(own, logs, other):
    vmem = pl.BlockSpec(memory_space=pltpu.VMEM)
    return pl.pallas_call(
        join_kernel,
        out_shape=jax.ShapeDtypeStruct((TOK, GROUP * HEAD), jnp.bfloat16),
        in_specs=[vmem] * 3,
        out_specs=vmem,
    )(own, logs, other)


def on_device(tokens, norm_gain, w_query, keyvalue_weight, cache_keyval, kept_blocks, kept_counts):
    me = lax.axis_index("wa").astype(jnp.int32)
    shard = lax.axis_index("ctx").astype(jnp.int32)
    z, y_hi, x = shard // 8, (shard // 4) % 2, shard % 4

    kept = [
        lax.dynamic_slice_in_dim(cache_keyval, kept_blocks[0, s] * BLOCK, BLOCK, 0) for s in range(MAXB)
    ]
    count_rows = jnp.broadcast_to(kept_counts[0].astype(jnp.bfloat16), (16, 2 * HEAD))
    kept_all = gather_plane(jnp.concatenate([*kept, count_rows], axis=0))
    counts = kept_all[:, MAXB * BLOCK, 0].astype(jnp.int32)

    values = tokens.astype(jnp.float32)
    sumsq = lax.psum(jnp.sum(values * values, axis=1, keepdims=True), "wa")
    send, keep = project(me.reshape(1), tokens, norm_gain, sumsq, w_query, keyvalue_weight)
    got = lax.ppermute(send, "wa", [(i, i ^ 1) for i in range(4)])
    chip = keep + got
    far = lax.ppermute(chip[0], "wa", [(i, i ^ 2) for i in range(4)])
    whole = chip[1] + far
    queries = (whole[:, : GROUP * HEAD] * HEAD ** (-0.5)).astype(jnp.bfloat16)
    new_keyval = whole[:, GROUP * HEAD :].astype(jnp.bfloat16)

    across = [(i, i ^ 4) for i in range(32)]
    other_queries = lax.ppermute(queries, "ctx", across)
    new_all = gather_plane(new_keyval).reshape(PEERS * TOK, 2 * HEAD)

    acc, top = attend_cached(counts, queries, other_queries, kept_all)
    info_other = jnp.stack([z + 1 - y_hi, x])
    (sent,) = attend_span(False, info_other, other_queries, new_all, acc, top)
    theirs = lax.ppermute(sent, "ctx", across)
    info_own = jnp.stack([z, x])
    own, logs = attend_span(True, info_own, queries, new_all, acc, top)
    return join(own, logs, theirs)


def solution(mesh):
    return jax.shard_map(
        on_device,
        mesh=mesh,
        in_specs=(
            P("ctx", "wa"),
            P("wa"),
            P("wa", None),
            P("wa", None),
            P("ctx", "wa"),
            P("ctx", None),
            P("ctx"),
        ),
        out_specs=P("ctx", "wa"),
        check_vma=False,
    )
```

time: 602 us -> 151 us (0.25)
  the two profiles are of different devices: /device:TPU:0 before, /device:TPU:96 now
where the time goes in v1:
time: 151 us
  waiting for transfers between devices  42 us (28%)
  Pallas kernels  41.9 us (28%)
  local copies, waits for them, and re-layouts  26 us (17%)
  starting transfers between devices  22.2 us (15%)
  blocking collectives  12 us (8%)
  other arithmetic  3.86 us (3%)
  between operations  2.83 us (2%)
    all_to_all x2, waiting for transfers between devices, gather_plane(): lax.all_to_all(copies, 'ctx', split_axis=0, concat_axis=0, axis_index_gro...  25.9 us
    unnamed x26, local copies, waits for them, and re-layouts  18.2 us
    pallas_call x1, Pallas kernels, attend_cached(): pl.pallas_call(cached_kernel, out_shape=(jax.ShapeDtypeStruct((rows, 2 *...  17.1 us
    ppermute x1, waiting for transfers between devices, on_device(): far = lax.ppermute(chip[0], 'wa', [(i, i ^ 2) for i in range(4)])  16.2 us
    pallas_call x2, Pallas kernels, attend_span(): pl.pallas_call(kernel, out_shape=outs, grid=(1,), in_specs=[pl.BlockSpec(...  13.1 us
    all_to_all x2, starting transfers between devices, gather_plane(): lax.all_to_all(copies, 'ctx', split_axis=0, concat_axis=0, axis_index_gro...  12.8 us
    psum x1, blocking collectives, on_device(): sumsq = lax.psum(jnp.sum(values * values, axis=1, keepdims=True), 'wa')  12 us
    pallas_call x1, Pallas kernels, project(): pl.pallas_call(project_kernel, out_shape=(shape, shape), grid_spec=pltpu....  8.77 us
  transfers between devices with their start and end apart: 6, of which 2 were waited for; matrix products, arithmetic and copies ran while one was open for 6% of the time, Pallas kernels for 15%

profile of v1, /device:TPU:96, one launch (start us, length us, event | category | flops | bytes accessed | tf_op | source)
XLA Modules:
  0.0 150.9 jit_solution(471073837222441586)
XLA Ops:
  0.0 1.2 multiply_reduce_fusion
  1.2 0.1 copy.9
  1.3 12.0 %psum.7.ss_ref = f32[128,1]{1,0:T(8,128)S(1)} all-reduce(f32[128,1]{1,0:T(8,128)S(1)} %copy.9), channel_id=1, replica_groups=mesh['ctx'=32,'wa'=4] {'wa'}, use_global_device_ids=true, to_apply=%region_1.2 | all-reduce | flops 128 | bytes 1024 | tf_op jit(solution)/shard_map/psum | solution.py:339
  13.4 0.7 reshape.21.gain_ref
  14.1 0.0 copy-start
  14.1 5.8 %copy-done = bf16[2048,4096]{1,0:T(8,128)(2,1)S(1)} copy-done((bf16[2048,4096]{1,0:T(8,128)(2,1)S(1)}, bf16[2048,4096]{1,0:T(8,128)(2,1)}, u32[]{:S(2)}) %copy-start) | copy-done | bytes 16777240
  19.9 0.0 copy-start.1
  19.9 2.2 %copy-done.1 = bf16[2048,1024]{1,0:T(8,128)(2,1)S(1)} copy-done((bf16[2048,1024]{1,0:T(8,128)(2,1)S(1)}, bf16[2048,1024]{1,0:T(8,128)(2,1)}, u32[]{:S(2)}) %copy-start.1) | copy-done | bytes 4194328
  22.1 0.0 copy-start.2
  22.1 1.0 copy-done.2
  23.1 0.0 copy-start.12
  23.1 8.8 %shard_map.73 = (f32[2,128,1280]{2,1,0:T(8,128)}, f32[2,128,1280]{2,1,0:T(8,128)S(1)}) custom-call(s32[1]{0:T(128)} %bitcast.2.me_ref, bf16[128,2048]{1,0:T(8,128)(2,1)S(1)} %copy-done.2, bf16[1,2048]{1,0:T(2,128)(2,1)S(1)} %reshape.21.gain_ref, f32[128,1]{1,0:T(8,128)S(1)} %psum.7.ss_ref, bf16[2048,4096]{1,0:T(8,128)(2,1)S(1)} %copy-done, ...), custom_call_target="tpu_custom_call" | custom-call | flops 2684354560 | bytes 25165824 | tf_op jit(solution)/shard_map/pallas_call | solution.py:67
  31.9 0.0 copy-start.3
  31.9 1.1 copy-done.3
  33.0 0.0 collective-permute-start
  33.0 0.0 copy-done.12
  33.0 0.7 fusion.3
  36.3 0.9 constant_dynamic-slice_fusion.2
  37.3 0.1 maximum_maximum_fusion
  37.4 1.9 %broadcast_in_dim.21 = bf16[16,400,256]{2,1,0:T(8,128)(2,1)} broadcast(bf16[400,256]{1,0:T(8,128)(2,1)S(1)} %maximum_maximum_fusion), dimensions={1,2} | broadcast | bytes 3481600 | tf_op jit(solution)/shard_map/broadcast_in_dim | solution.py:31
  39.3 7.0 %all-to-all-start.1 = ((bf16[16,400,256]{2,1,0:T(8,128)(2,1)}), bf16[16,400,256]{2,1,0:T(8,128)(2,1)S(1)}, u32[]{:S(2)}, u32[]{:S(2)}) async-start(bf16[16,400,256]{2,1,0:T(8,128)(2,1)} %broadcast_in_dim.21), calls=%async_computation.1 | async-start | bytes 6553600 | tf_op jit(solution)/shard_map/all_to_all | solution.py:32
  46.3 0.0 collective-permute-done
  46.3 1.9 %add.30 = f32[2,128,1280]{2,1,0:T(8,128)S(1)} add(f32[2,128,1280]{2,1,0:T(8,128)} %copy-done.3, f32[2,128,1280]{2,1,0:T(8,128)} %collective-permute-done) | non-fusion elementwise | flops 327680 | bytes 3932160 | tf_op jit(solution)/shard_map/add | solution.py:342
  48.2 0.5 collective-permute-start.1
  48.7 16.2 %collective-permute-done.1 = f32[128,1280]{1,0:T(8,128)S(1)} collective-permute-done((f32[128,1280]{1,0:T(8,128)S(1)}, f32[128,1280]{1,0:T(8,128)S(1)}, u32[]{:S(2)}, u32[]{:S(2)}) %collective-permute-start.1) | collective-permute-done | bytes 655392 | tf_op jit(solution)/shard_map/ppermute | solution.py:343
  64.9 0.1 fusion
  64.9 0.0 copy-start.10
  65.0 0.8 copy-done.10
  65.8 3.0 %collective-permute-start.2 = (bf16[128,1024]{1,0:T(8,128)(2,1)S(1)}, bf16[128,1024]{1,0:T(8,128)(2,1)}, u32[]{:S(2)}, u32[]{:S(2)}) collective-permute-start(bf16[128,1024]{1,0:T(8,128)(2,1)S(1)} %fusion.1.qo_ref.q_ref), channel_id=1, source_target_pairs={{0,16},{4,20},{8,24},{12,28},{16,0},{20,4},{24,8},{28,12},{32,48},... | collective-permute-start | bytes 786440 | tf_op jit(solution)/shard_map/ppermute | solution.py:349
  68.8 1.5 %slice.49 = bf16[128,256]{1,0:T(8,128)(2,1)} slice(f32[128,1280]{1,0:T(8,128)} %copy-done.10), slice={[0:128], [1024:1280]} | slice | bytes 131072 | tf_op jit(solution)/shard_map/slice | solution.py:346
  70.4 25.9 %all-to-all-done.1.kv_ref = bf16[16,400,256]{2,1,0:T(8,128)(2,1)S(1)} async-done(((bf16[16,400,256]{2,1,0:T(8,128)(2,1)}), bf16[16,400,256]{2,1,0:T(8,128)(2,1)S(1)}, u32[]{:S(2)}, u32[]{:S(2)}) %all-to-all-start.1) | async-done | bytes 3276832 | tf_op jit(solution)/shard_map/all_to_all | solution.py:32
  96.2 2.0 %broadcast_in_dim.9 = bf16[16,128,256]{2,1,0:T(8,128)(2,1)} broadcast(bf16[128,256]{1,0:T(8,128)(2,1)} %slice.49), dimensions={1,2} | broadcast | bytes 1114112 | tf_op jit(solution)/shard_map/broadcast_in_dim | solution.py:31
  98.2 5.8 %all-to-all-start = ((bf16[16,128,256]{2,1,0:T(8,128)(2,1)}), bf16[16,128,256]{2,1,0:T(8,128)(2,1)}, u32[]{:S(2)}, u32[]{:S(2)}) async-start(bf16[16,128,256]{2,1,0:T(8,128)(2,1)} %broadcast_in_dim.9), calls=%async_computation | async-start | bytes 2097152 | tf_op jit(solution)/shard_map/all_to_all | solution.py:32
  104.0 0.1 pad_add_fusion.1.info_ref
  104.0 0.4 fusion.2.counts_ref
  104.4 0.0 collective-permute-done.2.qp_ref.q_ref
  104.4 17.1 %shard_map.74 = (f32[2048,256]{1,0:T(8,128)S(1)}, f32[2048,128]{1,0:T(8,128)S(1)}) custom-call(s32[16]{0:T(128)S(1)} %fusion.2.counts_ref, bf16[128,1024]{1,0:T(8,128)(2,1)S(1)} %fusion.1.qo_ref.q_ref, bf16[128,1024]{1,0:T(8,128)(2,1)} %collective-permute-done.2.qp_ref.q_ref, bf16[16,400,256]{2,1,0:T(8,128)(2,1)S(1)} %all-to-all-done.1.kv_ref), custom_call_target="tpu_custom_call" | custom-call | flops 8589934592 | bytes 8388608 | tf_op jit(solution)/shard_map/pallas_call | solution.py:178
  121.5 0.0 copy-start.6
  121.5 1.3 copy-done.6
  122.9 0.0 copy-start.8
  122.9 1.0 copy-done.8
  123.8 0.0 all-to-all-done
  123.9 0.0 copy-start.7
  123.9 1.6 %copy-done.7 = f32[2048,256]{1,0:T(8,128)S(1)} copy-done((f32[2048,256]{1,0:T(8,128)S(1)}, f32[2048,256]{1,0:T(8,128)}, u32[]{:S(2)}) %copy-start.7) | copy-done | bytes 2097176
  125.4 0.0 copy-start.9
  125.4 1.2 copy-done.9
  126.7 6.8 %shard_map.76 = bf16[128,1152]{1,0:T(8,128)(2,1)S(1)} custom-call(s32[2]{0:T(128)S(1)} %pad_add_fusion.1.info_ref, bf16[128,1024]{1,0:T(8,128)(2,1)} %collective-permute-done.2.qp_ref.q_ref, bf16[2048,256]{1,0:T(8,128)(2,1)} %bitcast.6.kv_ref, f32[2048,256]{1,0:T(8,128)S(1)} %copy-done.7, f32[2048,128]{1,0:T(8,128)S(1)} %copy-done.9), custom_call_target="tpu_custom_call" | custom-call | flops 2147483648 | bytes 4194304 | tf_op jit(solution)/shard_map/pallas_call | solution.py:275
  133.5 6.0 %collective-permute-start.3 = (bf16[128,1152]{1,0:T(8,128)(2,1)S(1)}, bf16[128,1152]{1,0:T(8,128)(2,1)S(1)}, u32[]{:S(2)}, u32[]{:S(2)}) collective-permute-start(bf16[128,1152]{1,0:T(8,128)(2,1)S(1)} %shard_map.76), channel_id=1, source_target_pairs={{0,16},{4,20},{8,24},{12,28},{16,0},{20,4},{24,8},{28,12},{32,48},... | collective-permute-start | bytes 884744 | tf_op jit(solution)/shard_map/ppermute | solution.py:355
  139.5 0.1 pad_add_fusion.info_ref
  139.6 6.3 %shard_map.75 = (f32[128,1024]{1,0:T(8,128)S(1)}, f32[128,128]{1,0:T(8,128)S(1)}) custom-call(s32[2]{0:T(128)S(1)} %pad_add_fusion.info_ref, bf16[128,1024]{1,0:T(8,128)(2,1)S(1)} %fusion.1.qo_ref.q_ref, bf16[2048,256]{1,0:T(8,128)(2,1)} %bitcast.6.kv_ref, f32[2048,256]{1,0:T(8,128)S(1)} %copy-done.7, f32[2048,128]{1,0:T(8,128)S(1)} %copy-done.9), custom_call_target="tpu_custom_call" | custom-call | flops 2147483648 | bytes 4194304 | tf_op jit(solution)/shard_map/pallas_call | solution.py:275
  145.9 0.0 copy-start.4
  145.9 0.8 copy-done.4
  146.6 0.0 copy-start.5
  146.6 0.6 copy-done.5
  147.3 0.0 collective-permute-done.3.other_ref
  147.3 0.0 copy-start.11
  147.3 0.7 copy-done.11
  148.0 2.9 %shard_map.77 = bf16[128,1024]{1,0:T(8,128)(2,1)} custom-call(f32[128,1024]{1,0:T(8,128)} %copy-done.4, f32[128,128]{1,0:T(8,128)} %copy-done.5, bf16[128,1152]{1,0:T(8,128)(2,1)} %copy-done.11), custom_call_target="tpu_custom_call" | custom-call | tf_op jit(solution)/shard_map/pallas_call | solution.py:318
  (4 shorter events, 0.1 us)
Async XLA Ops:
  14.1 5.8 %copy-start = (bf16[2048,4096]{1,0:T(8,128)(2,1)S(1)}, bf16[2048,4096]{1,0:T(8,128)(2,1)}, u32[]{:S(2)}) copy-start(bf16[2048,4096]{1,0:T(8,128)(2,1)} %wq_ref.1) | copy-start | bytes 50331652
  19.9 2.2 %copy-start.1 = (bf16[2048,1024]{1,0:T(8,128)(2,1)S(1)}, bf16[2048,1024]{1,0:T(8,128)(2,1)}, u32[]{:S(2)}) copy-start(bf16[2048,1024]{1,0:T(8,128)(2,1)} %wkv_ref.1) | copy-start | bytes 12582916
  22.1 1.0 copy-start.2
  23.1 9.9 %copy-start.12 = (s32[1,3]{1,0:T(1,128)S(1)}, s32[1,3]{1,0:T(1,128)}, u32[]{:S(2)}) copy-start(s32[1,3]{1,0:T(1,128)} %param.12) | copy-start | bytes 40
  31.9 1.1 copy-start.3
  33.0 13.3 %collective-permute-start = (f32[2,128,1280]{2,1,0:T(8,128)}, f32[2,128,1280]{2,1,0:T(8,128)}, u32[]{:S(2)}, u32[]{:S(2)}) collective-permute-start(f32[2,128,1280]{2,1,0:T(8,128)} %get-tuple-element.12), channel_id=1, source_target_pairs={{0,1},{1,0},{2,3},{3,2},{4,5},{5,4},{6,7},{7,6},{8,9},{9,8},{10,11... | collective-permute-start | bytes 3932168 | tf_op jit(solution)/shard_map/ppermute | solution.py:341
  39.3 56.9 %all-to-all-start.1 = ((bf16[16,400,256]{2,1,0:T(8,128)(2,1)}), bf16[16,400,256]{2,1,0:T(8,128)(2,1)S(1)}, u32[]{:S(2)}, u32[]{:S(2)}) async-start(bf16[16,400,256]{2,1,0:T(8,128)(2,1)} %broadcast_in_dim.21), calls=%async_computation.1 | async-start | bytes 6553600 | tf_op jit(solution)/shard_map/all_to_all | solution.py:32
  48.2 16.7 %collective-permute-start.1 = (f32[128,1280]{1,0:T(8,128)S(1)}, f32[128,1280]{1,0:T(8,128)S(1)}, u32[]{:S(2)}, u32[]{:S(2)}) collective-permute-start(f32[128,1280]{1,0:T(8,128)S(1)} %slice_bitcast_fusion), channel_id=1, source_target_pairs={{0,2},{1,3},{2,0},{3,1},{4,6},{5,7},{6,4},{7,5},{8,10},{9,11},{10,... | collective-permute-start | bytes 1966088 | tf_op jit(solution)/shard_map/ppermute | solution.py:343
  64.9 0.8 copy-start.10
  65.8 38.6 %collective-permute-start.2 = (bf16[128,1024]{1,0:T(8,128)(2,1)S(1)}, bf16[128,1024]{1,0:T(8,128)(2,1)}, u32[]{:S(2)}, u32[]{:S(2)}) collective-permute-start(bf16[128,1024]{1,0:T(8,128)(2,1)S(1)} %fusion.1.qo_ref.q_ref), channel_id=1, source_target_pairs={{0,16},{4,20},{8,24},{12,28},{16,0},{20,4},{24,8},{28,12},{32,48},... | collective-permute-start | bytes 786440 | tf_op jit(solution)/shard_map/ppermute | solution.py:349
  98.2 25.7 %all-to-all-start = ((bf16[16,128,256]{2,1,0:T(8,128)(2,1)}), bf16[16,128,256]{2,1,0:T(8,128)(2,1)}, u32[]{:S(2)}, u32[]{:S(2)}) async-start(bf16[16,128,256]{2,1,0:T(8,128)(2,1)} %broadcast_in_dim.9), calls=%async_computation | async-start | bytes 2097152 | tf_op jit(solution)/shard_map/all_to_all | solution.py:32
  121.5 1.3 copy-start.6
  122.9 1.0 copy-start.8
  123.9 1.6 %copy-start.7 = (f32[2048,256]{1,0:T(8,128)S(1)}, f32[2048,256]{1,0:T(8,128)}, u32[]{:S(2)}) copy-start(f32[2048,256]{1,0:T(8,128)} %copy-done.6) | copy-start | bytes 6291460
  125.4 1.2 copy-start.9
  133.5 13.8 %collective-permute-start.3 = (bf16[128,1152]{1,0:T(8,128)(2,1)S(1)}, bf16[128,1152]{1,0:T(8,128)(2,1)S(1)}, u32[]{:S(2)}, u32[]{:S(2)}) collective-permute-start(bf16[128,1152]{1,0:T(8,128)(2,1)S(1)} %shard_map.76), channel_id=1, source_target_pairs={{0,16},{4,20},{8,24},{12,28},{16,0},{20,4},{24,8},{28,12},{32,48},... | collective-permute-start | bytes 884744 | tf_op jit(solution)/shard_map/ppermute | solution.py:355
  145.9 0.8 copy-start.4
  146.6 0.6 copy-start.5
  147.3 0.7 copy-start.11
